TPU v7x, 128 devices: a whole 4x4x4 slice. The times are simulated.
128 devices in a mesh: seq: 4 (over x), fsdp: 16 (over z, y), dp: 2 (over core).
Axes of the slice: x: 4, y: 4, z: 4, core: 2. Of those that a mesh axis runs over, the one named last changes fastest.
Arguments:
- layer_input: bfloat16 [32, 1024, 8192], P(('fsdp', 'dp'), 'seq'), may hold values from -6 to 6
- c_weight: bfloat16 [8192, 512], P('fsdp'), may hold values from -0.0625 to 0.0625
- head_input: bfloat16 [32, 1024, 8192], P(('fsdp', 'dp'), 'seq'), may hold values from -6 to 6
- b_input: bfloat16 [32, 1024, 512], P(('fsdp', 'dp'), 'seq'), may hold values from -0.1796875 to 0.1796875
- log_decay: float32 [32, 64, 1024], P(('fsdp', 'dp'), None, 'seq'), may hold values from -1 to 0
- skip_gain: float32 [64], replicated, may hold values from 0.5 to 2
- out_grad: bfloat16 [32, 1024, 8192], P(('fsdp', 'dp'), 'seq'), may hold values from -0.29882812 to 0.29882812
Outputs:
- head_input_grad: bfloat16 [32, 1024, 8192], P(('fsdp', 'dp'), 'seq')
- b_input_grad: bfloat16 [32, 1024, 512], P(('fsdp', 'dp'), 'seq')
- c_weight_grad: float32 [8192, 512], P('fsdp')
- log_decay_grad: float32 [32, 64, 1024], P(('fsdp', 'dp'), None, 'seq')
- skip_gain_grad: float32 [64], replicated
All inputs are finite; a program needn't handle non-finite values.
Results may differ from a plain program's by a relative error of at most 0.027.
Values may be sent and summed in bfloat16 or wider, within the bound.
A program may use at most 192 MiB of HBM per device.

v0:
```python
import jax
import jax.numpy as jnp
from jax import lax
from jax.sharding import PartitionSpec as P

HEAD_COUNT = 64
P_SIZE = 128
N = 128
G = 4
BLK = 256
HG = 16
HIGHEST = lax.Precision.HIGHEST


def entering_2(array, axis, combine, identity, reverse):
    peers, index = (lax.axis_size(axis), lax.axis_index(axis))
    everything = jax.tree.map(
        lambda part, kind: lax.all_gather(part.astype(kind), axis),
        array,
        (jnp.bfloat16, jnp.bfloat16),
    )
    start = jax.tree.map(
        lambda part, zero: jnp.broadcast_to(jnp.asarray(zero, part.dtype), part.shape),
        array,
        identity,
    )

    def turn(k, before):
        at = peers - 1 - k if reverse else k
        reached = at > index if reverse else at < index
        new = combine(
            before, jax.tree.map(lambda part, own: part[at].astype(own.dtype), everything, array)
        )
        return jax.tree.map(lambda a, b: jnp.where(reached, a, b), new, before)

    return lax.fori_loop(0, peers, turn, start)


def block_forward(values, b_block, c_block, log_block, skip_gain, entering):
    length = values.shape[0]
    running = jnp.cumsum(log_block, axis=1)
    ending = running[:, -1]
    spread = running[:, :, None] - running[:, None, :]
    causal = jnp.arange(length)[:, None] >= jnp.arange(length)[None, :]
    decays = jnp.exp(jnp.where(causal[None], spread, -1e30))
    b_groups = b_block.reshape(length, G, N)
    c_groups = c_block.reshape(length, G, N)
    scores = jnp.einsum("tgn,sgn->gts", c_groups, b_groups, preferred_element_type=jnp.float32)
    mixing = (decays.reshape(G, HG, length, length) * scores[:, None]).astype(jnp.bfloat16)
    grouped = values.reshape(length, G, HG, P_SIZE)
    within = jnp.einsum("gkts,sgkp->tgkp", mixing, grouped, preferred_element_type=jnp.float32)
    from_start = jnp.exp(running).T.reshape(length, G, HG, 1)
    c_decayed = c_groups[:, :, None, :].astype(jnp.float32) * from_start
    carried = jnp.einsum(
        "tgkn,gkpn->tgkp", c_decayed, entering.reshape(G, HG, P_SIZE, N), precision=HIGHEST
    )
    to_end = jnp.exp(ending[None, :] - running.T).reshape(length, G, HG, 1)
    b_decayed = (b_groups[:, :, None, :].astype(jnp.float32) * to_end).astype(jnp.bfloat16)
    own_state = jnp.einsum(
        "sgkp,sgkn->gkpn", grouped, b_decayed, preferred_element_type=jnp.float32
    )
    leaving = jnp.exp(ending)[:, None, None] * entering + own_state.reshape(HEAD_COUNT, P_SIZE, N)
    output = (
        within + carried + skip_gain.reshape(G, HG)[None, :, :, None] * grouped.astype(jnp.float32)
    )
    return (output.reshape(length, HEAD_COUNT * P_SIZE).astype(jnp.bfloat16), leaving)


def span_forward(values, b_span, c_span, log_span, skip_gain, entering):
    blocks_here = values.shape[0] // BLK
    pieces = (
        values.reshape(blocks_here, BLK, HEAD_COUNT * P_SIZE),
        b_span.reshape(blocks_here, BLK, G * N),
        c_span.reshape(blocks_here, BLK, G * N),
        jnp.moveaxis(log_span.reshape(HEAD_COUNT, blocks_here, BLK), 1, 0),
    )

    def advance(states, block_in):
        out_block, leaving = block_forward(
            block_in[0], block_in[1], block_in[2], block_in[3], skip_gain, states
        )
        return (leaving, out_block)

    leaving, outputs = lax.scan(advance, entering, pieces)
    return (outputs.reshape(values.shape[0], HEAD_COUNT * P_SIZE), leaving)


def span_summary(values, b_span, log_span):
    length = values.shape[0]
    running = jnp.cumsum(log_span, axis=1)
    ending = running[:, -1]
    to_end = jnp.exp(ending[None, :] - running.T).reshape(length, G, HG, 1)
    b_decayed = (b_span.reshape(length, G, 1, N).astype(jnp.float32) * to_end).astype(jnp.bfloat16)
    own_state = jnp.einsum(
        "sgkp,sgkn->gkpn",
        values.reshape(length, G, HG, P_SIZE),
        b_decayed,
        preferred_element_type=jnp.float32,
    )
    return (jnp.exp(ending), own_state.reshape(HEAD_COUNT, P_SIZE, N))


def span_adjoint(grad_span, c_span, log_span):
    length = grad_span.shape[0]
    running = jnp.cumsum(log_span, axis=1)
    from_start = jnp.exp(running).T.reshape(length, G, HG, 1)
    c_decayed = (c_span.reshape(length, G, 1, N).astype(jnp.float32) * from_start).astype(
        jnp.bfloat16
    )
    adjoint = jnp.einsum(
        "tgkp,tgkn->gkpn",
        grad_span.reshape(length, G, HG, P_SIZE),
        c_decayed,
        preferred_element_type=jnp.float32,
    )
    return adjoint.reshape(HEAD_COUNT, P_SIZE, N)


def chain_link(earlier, later):
    product = earlier[0] * later[0]
    combined = later[0][:, None, None] * earlier[1] + later[1]
    return (product, combined)


def on_device(layer_input, c_weight, head_input, b_input, log_decay, skip_gain, out_grad):
    tok_rows = layer_input[0]
    columns = tok_rows
    c_span = jnp.dot(
        columns,
        lax.all_gather(c_weight, "fsdp", axis=0, tiled=True),
        preferred_element_type=jnp.float32,
    ).astype(jnp.bfloat16)
    values = head_input[0]
    b_span = b_input[0]
    log_span = log_decay[0]
    grad_span = out_grad[0]
    span_decay, own_state = span_summary(values, b_span, log_span)
    decay_wire = span_decay.astype(jnp.bfloat16).astype(jnp.float32)
    own_wire = own_state.astype(jnp.bfloat16).astype(jnp.float32)
    adjoint_wire = (
        span_adjoint(grad_span, c_span, log_span).astype(jnp.bfloat16).astype(jnp.float32)
    )
    identity = (
        jnp.ones((HEAD_COUNT,), jnp.float32),
        jnp.zeros((HEAD_COUNT, P_SIZE, N), jnp.float32),
    )
    entering = entering_2((decay_wire, own_wire), "seq", chain_link, identity, False)[1]
    leaving_grad = entering_2((decay_wire, adjoint_wire), "seq", chain_link, identity, True)[1]
    entering = lax.optimization_barrier(entering.astype(jnp.bfloat16)).astype(jnp.float32)
    leaving_grad = lax.optimization_barrier(leaving_grad.astype(jnp.bfloat16)).astype(jnp.float32)
    primal, pullback = jax.vjp(span_forward, values, b_span, c_span, log_span, skip_gain, entering)
    values_grad, b_grad, c_grad, log_grad, skip_part, enter_grad = pullback(
        (grad_span, leaving_grad)
    )
    columns = tok_rows
    grad_shard = lax.psum_scatter(
        lax.dot_general(
            columns, c_grad, (((0,), (0,)), ((), ())), preferred_element_type=jnp.float32
        ).astype(jnp.bfloat16),
        "fsdp",
        scatter_dimension=0,
        tiled=True,
    )
    weight_grad = lax.psum(grad_shard, ("seq", "dp")).astype(jnp.float32)
    documents = lax.axis_size("fsdp") * lax.axis_size("dp")
    skip_total = lax.psum(skip_part, ("seq", "fsdp", "dp"))
    return (
        values_grad[None],
        b_grad[None],
        weight_grad / documents,
        log_grad[None],
        skip_total / documents,
    )


def solution(mesh):
    in_specs = (
        P(("fsdp", "dp"), "seq", None),
        P("fsdp", None),
        P(("fsdp", "dp"), "seq", None),
        P(("fsdp", "dp"), "seq", None),
        P(("fsdp", "dp"), None, "seq"),
        P(),
        P(("fsdp", "dp"), "seq", None),
    )
    out_specs = (
        P(("fsdp", "dp"), "seq", None),
        P(("fsdp", "dp"), "seq", None),
        P("fsdp", None),
        P(("fsdp", "dp"), None, "seq"),
        P(),
    )
    return jax.shard_map(
        on_device, mesh=mesh, in_specs=in_specs, out_specs=out_specs, check_vma=False
    )
```

profile of v0, /device:TPU:0, one launch (start us, length us, event | category | flops | bytes accessed | tf_op | source)
XLA Modules:
  0.0 422.4 jit_solution(13188554458518510789)
XLA Ops:
  11.2 3.6 copy.186
  14.8 4.8 %fusion.40 = bf16[4,16,128,128]{3,2,1,0:T(8,128)(2,1)S(1)} fusion(bf16[256,4,16,128]{3,2,1,0:T(8,128)(2,1)S(1)} %bitcast.145, f32[256,4,16]{0,2,1:T(8,128)S(1)} %bitcast.158, f32[256,4,128]{0,2,1:T(8,128)S(1)} %convert_element_type.256), kind=kOutput, calls=%fused_computation.57 | convolution fusion | flops 542113792 | bytes 6881280 | tf_op jit(solution)/shard_map/sgkp,sgkn->gkpn/dot_general | solution.py:94
  19.6 3.0 copy.166
  22.7 6.4 %copy.144 = bf16[1,256,8192]{1,2,0:T(8,128)(2,1)} copy(bf16[1,256,8192]{2,1,0:T(8,128)(2,1)} %param.17) | data formatting | bytes 8388608 | tf_op args[6]
  29.1 54.4 %all-gather.5.cloned.1.call-done = bf16[8192,512]{1,0:T(8,128)(2,1)} async-done(((bf16[512,512]{1,0:T(8,128)(2,1)}), bf16[8192,512]{1,0:T(8,128)(2,1)}) %all-gather.5.cloned.1.call-update) | async-done | bytes 8388624 | tf_op jit(solution)/shard_map/all_gather | solution.py:130
  83.5 7.0 %fusion.43 = bf16[256,512]{1,0:T(8,128)(2,1)S(1)} fusion(bf16[8192,512]{1,0:T(8,128)(2,1)} %all-gather.5.cloned.1.call-done, bf16[1,256,8192]{2,1,0:T(8,128)(2,1)} %param.11), kind=kOutput, calls=%fused_computation.60 | convolution fusion | flops 2147614720 | bytes 12845056 | tf_op jit(solution)/shard_map/dot_general | solution.py:128
  90.8 3.5 fusion.39
  94.2 2.9 copy.152
  99.5 10.7 %all-reduce.1 = bf16[256]{0:T(256)(128)(2,1)S(1)} all-reduce(bf16[256]{0:T(256)(128)(2,1)S(1)} %dynamic-update-slice), channel_id=2, replica_groups=mesh['seq'=4,'fsdp'=16,'dp'=2] {'seq'}, use_global_device_ids=true, to_apply=%add.1 | all-reduce | flops 256 | bytes 1024
  110.9 57.1 %all-gather.9.cloned.1.call-done = bf16[4,64,128,128]{3,2,1,0:T(8,128)(2,1)} async-done(((bf16[1,64,128,128]{3,2,1,0:T(8,128)(2,1)}), bf16[4,64,128,128]{3,2,1,0:T(8,128)(2,1)}) %all-gather.9.cloned.1.call-update) | async-done | bytes 8388624 | tf_op jit(solution)/shard_map/all_gather | solution.py:18
  168.1 23.4 %while.21 = (s32[]{:T(128)}, f32[64,128,128]{2,1,0:T(8,128)}, s32[]{:T(128)}, bf16[4,64]{1,0:T(4,128)(2,1)S(1)}, bf16[4,64,128,128]{3,2,1,0:T(8,128)(2,1)}, /*index=5*/s32[]{:T(128)}, s32[]{:T(128)}) while((s32[]{:T(128)}, f32[64,128,128]{2,1,0:T(8,128)}, s32[]{:T(128)}, bf16[4,64]{1,0:T(4,128)(2,1)S(1)}, ...), condition=%wide.region_7.8_spmd.clone, body=%wide.region_6.7_spmd.clone.sunk | while | flops 5242948 | bytes 10486513 | solution.py:36
  168.1 4.6 %fusion.74 = f32[64,128,128]{2,1,0:T(8,128)} fusion(f32[64,128,128]{2,1,0:T(8,128)} %get-tuple-element.601, bf16[4,64,128,128]{3,2,1,0:T(8,128)(2,1)} %get-tuple-element.611, s32[]{:T(128)S(6)} %copy.210, f32[64]{0:T(128)S(1)} %bitcast_convert_fusion.5, pred[]{:T(512)S(6)} %compare.8, pred[]{:T(512)S(6)} %lt.47), kind=kLoop, calls=%fused_computation.4.clone.1 | loop fusion | flops 5242880 | bytes 10486022 | tf_op jit(solution)/shard_map/while/body/eval_jaxpr/jit(_where)/select_n | solution.py:34
  172.7 5.9 %fusion.74 = f32[64,128,128]{2,1,0:T(8,128)} fusion(f32[64,128,128]{2,1,0:T(8,128)} %get-tuple-element.601, bf16[4,64,128,128]{3,2,1,0:T(8,128)(2,1)} %get-tuple-element.611, s32[]{:T(128)S(6)} %copy.210, f32[64]{0:T(128)S(1)} %bitcast_convert_fusion.5, pred[]{:T(512)S(6)} %compare.8, pred[]{:T(512)S(6)} %lt.47), kind=kLoop, calls=%fused_computation.4.clone.1 | loop fusion | flops 5242880 | bytes 10486022 | tf_op jit(solution)/shard_map/while/body/eval_jaxpr/jit(_where)/select_n | solution.py:34
  178.6 6.7 %fusion.74 = f32[64,128,128]{2,1,0:T(8,128)} fusion(f32[64,128,128]{2,1,0:T(8,128)} %get-tuple-element.601, bf16[4,64,128,128]{3,2,1,0:T(8,128)(2,1)} %get-tuple-element.611, s32[]{:T(128)S(6)} %copy.210, f32[64]{0:T(128)S(1)} %bitcast_convert_fusion.5, pred[]{:T(512)S(6)} %compare.8, pred[]{:T(512)S(6)} %lt.47), kind=kLoop, calls=%fused_computation.4.clone.1 | loop fusion | flops 5242880 | bytes 10486022 | tf_op jit(solution)/shard_map/while/body/eval_jaxpr/jit(_where)/select_n | solution.py:34
  185.4 6.1 %fusion.74 = f32[64,128,128]{2,1,0:T(8,128)} fusion(f32[64,128,128]{2,1,0:T(8,128)} %get-tuple-element.601, bf16[4,64,128,128]{3,2,1,0:T(8,128)(2,1)} %get-tuple-element.611, s32[]{:T(128)S(6)} %copy.210, f32[64]{0:T(128)S(1)} %bitcast_convert_fusion.5, pred[]{:T(512)S(6)} %compare.8, pred[]{:T(512)S(6)} %lt.47), kind=kLoop, calls=%fused_computation.4.clone.1 | loop fusion | flops 5242880 | bytes 10486022 | tf_op jit(solution)/shard_map/while/body/eval_jaxpr/jit(_where)/select_n | solution.py:34
  191.4 2.6 convert_element_type.274
  194.6 5.0 %fusion.10 = (f32[256,4,16]{0,2,1:T(8,128)}, bf16[256,4,128]{0,2,1:T(8,128)(2,1)S(1)}) fusion(f32[256,4,128]{0,2,1:T(8,128)S(1)} %copy.148, f32[256,4,16]{0,2,1:T(8,128)} %bitcast.162, bf16[4,16,128,128]{3,2,1,0:T(8,128)(2,1)S(1)} %bitcast.134, bf16[4,16,128,256]{3,2,1,0:T(8,128)(2,1)} %bitcast.141), kind=kOutput, calls=%fused_computation.21 | convolution fusion | flops 545112064 | bytes 7208960 | tf_op jit(solution)/shard_map/transpose(jvp())/while/body/eval_jaxpr/tgkn,gkpn->tgkp/dot_general | solution.py:54
  199.8 18.1 %fusion.6 = (f32[4,16,256]{2,1,0:T(8,128)}, f32[4,16,256]{2,1,0:T(8,128)}, bf16[4,256,256]{2,1,0:T(8,128)(2,1)S(1)}) fusion(f32[4,256,256]{2,1,0:T(8,128)S(1)} %fusion.55, f32[4,16,256]{2,1,0:T(8,128)S(1)} %copy-done.17, pred[256,256]{1,0:T(8,128)(4,1)S(1)} %copy-done.19, bf16[4,16,128,256]{3,2,1,0:T(8,128)(2,1)S(1)} %bitcast.144, ...), kind=kOutput, calls=%fused_computation.14 | convolution fusion | flops 1119584256 | bytes 10223616 | tf_op jit(solution)/shard_map/transpose(jvp())/while/body/eval_jaxpr/gkts,sgkp->tgkp/dot_general | solution.py:51
  218.2 5.6 %fusion.7 = bf16[8192,512]{0,1:T(8,128)(2,1)} fusion(bf16[256,512]{0,1:T(8,128)(2,1)S(1)} %bitcast.153, bf16[1,256,8192]{2,1,0:T(8,128)(2,1)S(1)} %copy-done.1), kind=kOutput, calls=%fused_computation.16 | convolution fusion | flops 2151677952 | bytes 12845056 | tf_op jit(solution)/shard_map/dot_general | solution.py:157
  224.5 4.9 %multiply_reduce_fusion = f32[8192]{0:T(1024)S(1)} fusion(bf16[1,256,8192]{2,1,0:T(8,128)(2,1)} %param.13, bf16[1,256,8192]{2,1,0:T(8,128)(2,1)} %param.17), kind=kLoop, calls=%fused_computation.26 | loop fusion | flops 8380416 | bytes 8421376 | tf_op jit(solution)/shard_map/transpose(jvp())/while/body/eval_jaxpr/reduce_sum | solution.py:64
  229.7 67.1 %psum.15 = f32[64]{0:T(128)S(1)} all-reduce(f32[64]{0:T(128)S(1)} %reshape.375), channel_id=1, replica_groups=mesh['seq'=4,'fsdp'=16,'dp'=2] {'seq','fsdp','dp'}, use_global_device_ids=true, to_apply=%region_21.22 | all-reduce | flops 64 | bytes 512 | tf_op jit(solution)/shard_map/psum | solution.py:166
  299.6 7.3 %fusion.8 = bf16[4,16,256,128]{2,3,1,0:T(8,128)(2,1)} fusion(bf16[4,16,128,256]{3,2,1,0:T(8,128)(2,1)} %bitcast.142, f32[4,256,256]{2,1,0:T(8,128)} %copy-done.6, f32[4,16,256]{2,1,0:T(8,128)S(1)} %copy-done.18, pred[256,256]{1,0:T(8,128)(4,1)S(1)} %copy-done.20), kind=kOutput, calls=%fused_computation.17 | convolution fusion | flops 1090519040 | bytes 9568256 | tf_op jit(solution)/shard_map/transpose(jvp())/while/body/eval_jaxpr/gkts,sgkp->tgkp/dot_general | solution.py:51
  306.9 22.8 %while.20 = (s32[]{:T(128)}, f32[64,128,128]{2,1,0:T(8,128)}, s32[]{:T(128)}, bf16[4,64]{1,0:T(4,128)(2,1)S(1)}, bf16[4,64,128,128]{3,2,1,0:T(8,128)(2,1)}, /*index=5*/s32[]{:T(128)}, s32[]{:T(128)}, s32[]{:T(128)}, s32[]{:T(128)}) while((s32[]{:T(128)}, f32[64,128,128]{2,1,0:T(8,128)}, s32[]{:T(128)}, ...), condition=%wide.region_3.4_spmd.clone, body=%wide.region_2.3_spmd.clone.sunk | while | flops 5242952 | bytes 10486575 | solution.py:36
  306.9 4.8 %fusion.73 = f32[64,128,128]{2,1,0:T(8,128)} fusion(f32[64,128,128]{2,1,0:T(8,128)} %get-tuple-element.576, bf16[4,64,128,128]{3,2,1,0:T(8,128)(2,1)} %get-tuple-element.588, s32[]{:T(128)S(6)} %select_n.103, f32[64]{0:T(128)S(1)} %bitcast_convert_fusion.4, pred[]{:T(512)S(6)} %compare.7, pred[]{:T(512)S(6)} %gt.12), kind=kLoop, calls=%fused_computation.1.clone.1 | loop fusion | flops 5242880 | bytes 10486022 | tf_op jit(solution)/shard_map/while/body/eval_jaxpr/jit(_where)/select_n | solution.py:34
  311.7 6.0 %fusion.73 = f32[64,128,128]{2,1,0:T(8,128)} fusion(f32[64,128,128]{2,1,0:T(8,128)} %get-tuple-element.576, bf16[4,64,128,128]{3,2,1,0:T(8,128)(2,1)} %get-tuple-element.588, s32[]{:T(128)S(6)} %select_n.103, f32[64]{0:T(128)S(1)} %bitcast_convert_fusion.4, pred[]{:T(512)S(6)} %compare.7, pred[]{:T(512)S(6)} %gt.12), kind=kLoop, calls=%fused_computation.1.clone.1 | loop fusion | flops 5242880 | bytes 10486022 | tf_op jit(solution)/shard_map/while/body/eval_jaxpr/jit(_where)/select_n | solution.py:34
  317.7 6.0 %fusion.73 = f32[64,128,128]{2,1,0:T(8,128)} fusion(f32[64,128,128]{2,1,0:T(8,128)} %get-tuple-element.576, bf16[4,64,128,128]{3,2,1,0:T(8,128)(2,1)} %get-tuple-element.588, s32[]{:T(128)S(6)} %select_n.103, f32[64]{0:T(128)S(1)} %bitcast_convert_fusion.4, pred[]{:T(512)S(6)} %compare.7, pred[]{:T(512)S(6)} %gt.12), kind=kLoop, calls=%fused_computation.1.clone.1 | loop fusion | flops 5242880 | bytes 10486022 | tf_op jit(solution)/shard_map/while/body/eval_jaxpr/jit(_where)/select_n | solution.py:34
  323.7 5.9 %fusion.73 = f32[64,128,128]{2,1,0:T(8,128)} fusion(f32[64,128,128]{2,1,0:T(8,128)} %get-tuple-element.576, bf16[4,64,128,128]{3,2,1,0:T(8,128)(2,1)} %get-tuple-element.588, s32[]{:T(128)S(6)} %select_n.103, f32[64]{0:T(128)S(1)} %bitcast_convert_fusion.4, pred[]{:T(512)S(6)} %compare.7, pred[]{:T(512)S(6)} %gt.12), kind=kLoop, calls=%fused_computation.1.clone.1 | loop fusion | flops 5242880 | bytes 10486022 | tf_op jit(solution)/shard_map/while/body/eval_jaxpr/jit(_where)/select_n | solution.py:34
  329.7 2.7 convert_element_type.255
  333.2 6.1 %fusion.12 = (f32[256,4,16]{0,2,1:T(8,128)}, bf16[256,4,128]{0,2,1:T(8,128)(2,1)}) fusion(f32[256,4,128]{0,2,1:T(8,128)S(1)} %copy-done.8, f32[256,4,16]{0,2,1:T(8,128)S(1)} %bitcast.160, bf16[4,16,128,128]{3,2,1,0:T(8,128)(2,1)S(1)} %bitcast.135, bf16[256,4,16,128]{3,2,1,0:T(8,128)(2,1)S(1)} %bitcast.147), kind=kOutput, calls=%fused_computation.25 | convolution fusion | flops 549306368 | bytes 7208960 | tf_op jit(solution)/shard_map/transpose(jvp())/while/body/eval_jaxpr/sgkp,sgkn->gkpn/dot_general | solution.py:59
  346.7 8.7 %fusion.21 = bf16[256,4,16,128]{0,3,2,1:T(8,128)(2,1)} fusion(bf16[256,4,16,128]{0,3,2,1:T(8,128)(2,1)} %bitcast.143, bf16[4,16,256,128]{2,3,1,0:T(8,128)(2,1)} %fusion.8, f32[4,16]{1,0:T(4,128)S(1)} %mul.237, bf16[4,16,128,128]{3,2,1,0:T(8,128)(2,1)} %bitcast.136, f32[256,4,16]{0,2,1:T(8,128)} %bitcast.159, f32[256,4,128]{0,2,1:T(8,128)} %copy-done.7), kind=kOutput, calls=%fused_computation.39 | convolution fusion | flops 553648128 | bytes 15270144 | tf_op jit(solution)/shard_map/transpose(jvp())/while/body/eval_jaxpr/sgkp,sgkn->gkpn/dot_general | solution.py:59
  355.5 6.3 %copy.175 = bf16[1,256,8192]{2,1,0:T(8,128)(2,1)} copy(bf16[1,256,8192]{1,2,0:T(8,128)(2,1)} %bitcast.148) | data formatting | bytes 8388608
  363.6 49.8 %all-reduce.4.cloned.1.call-done = bf16[512,512]{0,1:T(8,128)(2,1)} async-done(((bf16[512,512]{0,1:T(8,128)(2,1)}), bf16[512,512]{0,1:T(8,128)(2,1)}) %all-reduce.4.cloned.1.call-update) | async-done | bytes 524304 | tf_op jit(solution)/shard_map/psum | solution.py:164
  (121 shorter events, 23.8 us)
Async XLA Ops:
  7.2 76.3 %all-gather.5.cloned.1.call-start = ((), (), s32[]{:S(2)}) async-start(), calls=%async_computation.1 | async-start | bytes 8912896 | tf_op jit(solution)/shard_map/all_gather | solution.py:130
  7.9 160.2 %all-gather.9.cloned.1.call-start = ((), (), s32[]{:S(2)}) async-start(), calls=%async_computation.3 | async-start | bytes 10485760 | tf_op jit(solution)/shard_map/all_gather | solution.py:18
  11.1 3.7 copy-start.12
  11.2 3.6 copy-start.7
  14.7 4.9 %copy-start.3 = (bf16[32,8,64,128]{3,2,1,0:T(8,128)(2,1)}, bf16[32,8,64,128]{3,2,1,0:T(8,128)(2,1)S(1)}, u32[]{:S(2)}) copy-start(bf16[32,8,64,128]{3,2,1,0:T(8,128)(2,1)S(1)} %copy.186) | copy-start | bytes 12582916
  22.6 284.3 %all-gather.7.cloned.1.call-start = ((), (), s32[]{:S(2)}) async-start(), calls=%async_computation.2 | async-start | bytes 10485760 | tf_op jit(solution)/shard_map/all_gather | solution.py:18
  29.1 61.6 %copy-start.14 = (f32[256,64]{0,1:T(8,128)}, f32[256,64]{0,1:T(8,128)S(1)}, u32[]{:S(2)}) copy-start(f32[256,64]{0,1:T(8,128)S(1)} %copy.150) | copy-start | bytes 196612
  94.2 3.8 copy-start.23
  97.2 258.2 %reduce-scatter.2.cloned.1.call-start = ((), (), s32[]{:S(2)}) async-start(), calls=%async_computation.4 | async-start | bytes 8912896 | tf_op jit(solution)/shard_map/reduce_scatter | solution.py:156
  194.6 5.1 %copy-start.6 = (f32[4,256,256]{2,1,0:T(8,128)}, f32[4,256,256]{2,1,0:T(8,128)S(1)}, u32[]{:S(2)}) copy-start(f32[4,256,256]{2,1,0:T(8,128)S(1)} %fusion.55) | copy-start | bytes 3145732
  194.6 5.1 %copy-start.2 = (bf16[1,256,8192]{1,2,0:T(8,128)(2,1)S(1)}, bf16[1,256,8192]{1,2,0:T(8,128)(2,1)}, u32[]{:S(2)}) copy-start(bf16[1,256,8192]{1,2,0:T(8,128)(2,1)} %copy.144) | copy-start | bytes 12582916
  194.6 5.2 %copy-start.4 = (bf16[32,8,64,128]{3,2,1,0:T(8,128)(2,1)S(1)}, bf16[32,8,64,128]{3,2,1,0:T(8,128)(2,1)}, u32[]{:S(2)}) copy-start(bf16[32,8,64,128]{3,2,1,0:T(8,128)(2,1)} %copy-done.3) | copy-start | bytes 12582916
  194.6 5.2 %copy-start.17 = (f32[4,16,256]{2,1,0:T(8,128)S(1)}, f32[4,16,256]{2,1,0:T(8,128)}, u32[]{:S(2)}) copy-start(f32[4,16,256]{2,1,0:T(8,128)} %reduce_window_sum.59) | copy-start | bytes 196612
  194.6 5.1 %copy-start.19 = (pred[256,256]{1,0:T(8,128)(4,1)S(1)}, pred[256,256]{1,0:T(8,128)(4,1)}, u32[]{:S(2)}) copy-start(pred[256,256]{1,0:T(8,128)(4,1)} %iota_compare_fusion) | copy-start | bytes 196612
  199.8 18.4 %copy-start.1 = (bf16[1,256,8192]{2,1,0:T(8,128)(2,1)S(1)}, bf16[1,256,8192]{2,1,0:T(8,128)(2,1)}, u32[]{:S(2)}) copy-start(bf16[1,256,8192]{2,1,0:T(8,128)(2,1)} %param.11) | copy-start | bytes 12582916
  223.8 0.7 copy-start.22
  223.8 189.6 %all-reduce.4.cloned.1.call-start = ((), (), s32[]{:S(2)}) async-start(), calls=%async_computation.5 | async-start | bytes 1048576 | tf_op jit(solution)/shard_map/psum | solution.py:164
  224.5 72.8 %copy-start.16 = (f32[4,16,256]{2,1,0:T(8,128)S(1)}, f32[4,16,256]{2,1,0:T(8,128)}, u32[]{:S(2)}) copy-start(f32[4,16,256]{2,1,0:T(8,128)} %get-tuple-element.474) | copy-start | bytes 196612
  224.5 73.5 %copy-start.21 = (f32[4,16,256]{2,1,0:T(8,128)S(1)}, f32[4,16,256]{2,1,0:T(8,128)}, u32[]{:S(2)}) copy-start(f32[4,16,256]{2,1,0:T(8,128)} %get-tuple-element.473) | copy-start | bytes 196612
  224.5 74.3 %copy-start.15 = (f32[256,4,16]{0,2,1:T(8,128)S(1)}, f32[256,4,16]{0,2,1:T(8,128)}, u32[]{:S(2)}) copy-start(f32[256,4,16]{0,2,1:T(8,128)} %get-tuple-element.476) | copy-start | bytes 196612
  224.5 75.1 %copy-start.18 = (f32[4,16,256]{2,1,0:T(8,128)S(1)}, f32[4,16,256]{2,1,0:T(8,128)}, u32[]{:S(2)}) copy-start(f32[4,16,256]{2,1,0:T(8,128)} %reduce_window_sum.59) | copy-start | bytes 196612
  224.5 75.1 %copy-start.20 = (pred[256,256]{1,0:T(8,128)(4,1)S(1)}, pred[256,256]{1,0:T(8,128)(4,1)}, u32[]{:S(2)}) copy-start(pred[256,256]{1,0:T(8,128)(4,1)} %iota_compare_fusion) | copy-start | bytes 196612
  329.7 3.4 copy-start.5
  329.7 3.6 copy-start.8
  329.7 3.6 copy-start.13
  332.4 6.9 %copy-start = (bf16[64,128,128]{2,1,0:T(8,128)(2,1)}, bf16[64,128,128]{2,1,0:T(8,128)(2,1)S(1)}, u32[]{:S(2)}) copy-start(bf16[64,128,128]{2,1,0:T(8,128)(2,1)S(1)} %convert_element_type.255) | copy-start | bytes 6291460
  339.3 3.5 copy-start.9
  339.3 3.5 copy-start.10
  339.3 3.5 copy-start.11
Sparse Core Ops, SparseCore 0:
  10.1 73.3 all-gather.4
  85.2 82.8 all-gather.8
  169.7 84.7 all-gather.6
  257.8 86.5 reduce-scatter.1
  355.5 57.8 all-reduce.3
where the time goes:
time: 423 us; the launch traced here: 422 us
  waiting for transfers between devices  162 us (38%)
  blocking collectives  77.8 us (18%)
  matrix products  67.9 us (16%)
  other arithmetic  64.8 us (15%)
  local copies, waits for them, and re-layouts  34.7 us (8%)
  between operations  14.9 us (4%)
    psum x1, blocking collectives, on_device(): skip_total = lax.psum(skip_part, ('seq', 'fsdp', 'dp'))  67.1 us
    all_gather x2, waiting for transfers between devices, entering_2(): lax.all_gather(part.astype(kind), axis)  57.1 us
    all_gather x1, waiting for transfers between devices, on_device(): lax.all_gather(c_weight, 'fsdp', axis=0, tiled=True)  54.4 us
    psum x1, waiting for transfers between devices, on_device(): weight_grad = lax.psum(grad_shard, ('seq', 'dp')).astype(jnp.float32)  49.8 us
    select_n x8, other arithmetic, turn(): return jax.tree.map(lambda a, b: jnp.where(reached, a, b), new, before)  46.1 us
    dot_general x2, matrix products, block_forward(): jnp.einsum('gkts,sgkp->tgkp', mixing, grouped, preferred_element_type=jnp...  25.4 us
    unnamed x56, local copies, waits for them, and re-layouts  20.9 us
    dot_general x2, matrix products, block_forward(): jnp.einsum('sgkp,sgkn->gkpn', grouped, b_decayed, preferred_element_type=...  14.8 us
  transfers between devices with their start and end apart: 5, of which 3 were waited for; matrix products, arithmetic and copies ran while one was open for 39% of the time, Pallas kernels for 0%

commit v1 on v0

--- a/solution.py
+++ b/solution.py
@@ -10,6 +10,13 @@
 BLK = 256
 HG = 16
 HIGHEST = lax.Precision.HIGHEST
+
+
+def begin_the_domain(view):
+    val = lax.axis_size("fsdp")
+    block_out = jnp.stack(val * [view], axis=0)
+    main = lax.all_to_all(block_out, axis_name="fsdp", split_axis=0, concat_axis=0)
+    return jnp.concatenate(main, 0)
 
 
 def entering_2(array, axis, combine, identity, reverse):
@@ -126,9 +133,7 @@
     tok_rows = layer_input[0]
     columns = tok_rows
     c_span = jnp.dot(
-        columns,
-        lax.all_gather(c_weight, "fsdp", axis=0, tiled=True),
-        preferred_element_type=jnp.float32,
+        columns, begin_the_domain(c_weight), preferred_element_type=jnp.float32
     ).astype(jnp.bfloat16)
     values = head_input[0]
     b_span = b_input[0]

time: 423 us -> 452 us (1.069); the launches traced: 422 us -> 443 us
  starting transfers between devices: 0.2 us -> 8.35 us
  waiting for transfers between devices: 162 us -> 168 us
  blocking collectives: 77.8 us -> 83.6 us
    all_to_all x0 -> x1, waiting for transfers between devices: none -> 117 us  [begin_the_domain(): lax.all_to_all(block_out, axis_name='fsdp', split_axis=0, concat_axis=0)]
    all_gather x2, waiting for transfers between devices: 57.1 us -> 0.02 us  [entering_2(): lax.all_gather(part.astype(kind), axis)]
    all_gather x1 -> x0, waiting for transfers between devices: 54.4 us -> none  [on_device(): lax.all_gather(c_weight, 'fsdp', axis=0, tiled=True)]
    unnamed x1, blocking collectives: 10.7 us -> 20.8 us
    all_to_all x0 -> x1, starting transfers between devices: none -> 8.18 us  [begin_the_domain(): lax.all_to_all(block_out, axis_name='fsdp', split_axis=0, concat_axis=0)]
    unnamed x56 -> x42, local copies, waits for them, and re-layouts: 20.9 us -> 22.7 us
  transfers between devices with their start and end apart: 5 -> 5, of which waited for: 3 -> 2; matrix products, arithmetic and copies ran while one was open for 39% -> 33% of each run, Pallas kernels for 0% -> 0%
where the time goes in v1:
time: 452 us; the launch traced here: 443 us
  waiting for transfers between devices  168 us (37%)
  blocking collectives  83.6 us (18%)
  matrix products  65.4 us (14%)
  other arithmetic  63.7 us (14%)
  local copies, waits for them, and re-layouts  39.1 us (9%)
  between operations  15.2 us (3%)
  starting transfers between devices  8.35 us (2%)
    all_to_all x1, waiting for transfers between devices, begin_the_domain(): lax.all_to_all(block_out, axis_name='fsdp', split_axis=0, concat_axis=0)  117 us
    psum x1, blocking collectives, on_device(): skip_total = lax.psum(skip_part, ('seq', 'fsdp', 'dp'))  62.8 us
    psum x1, waiting for transfers between devices, on_device(): weight_grad = lax.psum(grad_shard, ('seq', 'dp')).astype(jnp.float32)  50.2 us
    select_n x8, other arithmetic, turn(): return jax.tree.map(lambda a, b: jnp.where(reached, a, b), new, before)  45.5 us
    dot_general x2, matrix products, block_forward(): jnp.einsum('gkts,sgkp->tgkp', mixing, grouped, preferred_element_type=jnp...  23.8 us
    unnamed x42, local copies, waits for them, and re-layouts  22.7 us
    unnamed x1, blocking collectives  20.8 us
    dot_general x2, matrix products, block_forward(): jnp.einsum('sgkp,sgkn->gkpn', grouped, b_decayed, preferred_element_type=...  14.7 us
  transfers between devices with their start and end apart: 5, of which 2 were waited for; matrix products, arithmetic and copies ran while one was open for 33% of the time, Pallas kernels for 0%

profile of v1, /device:TPU:0, one launch (start us, length us, event | category | flops | bytes accessed | tf_op | source)
XLA Modules:
  0.0 442.9 jit_solution(14334928876590309955)
XLA Ops:
  10.4 3.6 copy.186
  14.0 4.8 %fusion.40 = bf16[4,16,128,128]{3,2,1,0:T(8,128)(2,1)S(1)} fusion(bf16[256,4,16,128]{3,2,1,0:T(8,128)(2,1)S(1)} %bitcast.146, f32[256,4,16]{0,2,1:T(8,128)S(1)} %bitcast.159, f32[256,4,128]{0,2,1:T(8,128)S(1)} %convert_element_type.256), kind=kOutput, calls=%fused_computation.57 | convolution fusion | flops 542113792 | bytes 6881280 | tf_op jit(solution)/shard_map/sgkp,sgkn->gkpn/dot_general | solution.py:101
  18.9 2.9 copy.166
  21.9 4.0 stack.2
  25.9 8.2 %all-to-all-start = ((bf16[16,512,512]{2,1,0:T(8,128)(2,1)}), bf16[16,512,512]{2,1,0:T(8,128)(2,1)}, u32[]{:S(2)}, u32[]{:S(2)}) async-start(bf16[16,512,512]{2,1,0:T(8,128)(2,1)} %stack.2), calls=%async_computation | async-start | bytes 16777216 | tf_op jit(solution)/shard_map/all_to_all | solution.py:18
  34.1 6.6 %copy.144 = bf16[1,256,8192]{1,2,0:T(8,128)(2,1)} copy(bf16[1,256,8192]{2,1,0:T(8,128)(2,1)} %param.17) | data formatting | bytes 8388608 | tf_op args[6]
  40.8 117.3 %all-to-all-done = bf16[16,512,512]{2,1,0:T(8,128)(2,1)} async-done(((bf16[16,512,512]{2,1,0:T(8,128)(2,1)}), bf16[16,512,512]{2,1,0:T(8,128)(2,1)}, u32[]{:S(2)}, u32[]{:S(2)}) %all-to-all-start) | async-done | bytes 8388640 | tf_op jit(solution)/shard_map/all_to_all | solution.py:18
  158.1 7.0 %fusion.43 = bf16[256,512]{1,0:T(8,128)(2,1)S(1)} fusion(bf16[8192,512]{1,0:T(8,128)(2,1)} %bitcast.4, bf16[1,256,8192]{2,1,0:T(8,128)(2,1)} %param.11), kind=kOutput, calls=%fused_computation.60 | convolution fusion | flops 2147614720 | bytes 12845056 | tf_op jit(solution)/shard_map/dot_general | solution.py:135
  165.4 5.0 %fusion.39 = bf16[4,16,128,128]{3,2,1,0:T(8,128)(2,1)} fusion(bf16[256,4,16,128]{0,3,2,1:T(8,128)(2,1)} %bitcast.141, f32[256,4,16]{0,2,1:T(8,128)S(1)} %bitcast.162, f32[256,4,128]{0,2,1:T(8,128)S(1)} %copy.148), kind=kOutput, calls=%fused_computation.56 | convolution fusion | flops 542113792 | bytes 6881280 | tf_op jit(solution)/shard_map/tgkp,tgkn->gkpn/dot_general | solution.py:117
  170.4 4.1 copy.152
  176.2 20.8 %all-reduce.1 = bf16[256]{0:T(256)(128)(2,1)S(1)} all-reduce(bf16[256]{0:T(256)(128)(2,1)S(1)} %dynamic-update-slice), channel_id=2, replica_groups=mesh['seq'=4,'fsdp'=16,'dp'=2] {'seq'}, use_global_device_ids=true, to_apply=%add.1 | all-reduce | flops 256 | bytes 1024
  198.6 16.5 %fusion.6 = (f32[4,16,256]{2,1,0:T(8,128)}, f32[4,16,256]{2,1,0:T(8,128)S(1)}, bf16[4,256,256]{2,1,0:T(8,128)(2,1)S(1)}) fusion(f32[4,256,256]{2,1,0:T(8,128)S(1)} %fusion.55, f32[4,16,256]{2,1,0:T(8,128)S(1)} %reduce_window_sum.59, pred[256,256]{1,0:T(8,128)(4,1)S(1)} %iota_compare_fusion, bf16[4,16,128,256]{3,2,1,0:T(8,128)(2,1)} %bitcast.142, ...), kind=kOutput, calls=%fused_computation.14 | convolution fusion | flops 1119584256 | bytes 10223616 | tf_op jit(solution)/shard_map/transpose(jvp())/while/body/eval_jaxpr/gkts,sgkp->tgkp/dot_general | solution.py:58
  215.1 22.5 %while.21 = (s32[]{:T(128)}, f32[64,128,128]{2,1,0:T(8,128)}, s32[]{:T(128)}, bf16[4,64]{1,0:T(4,128)(2,1)S(1)}, bf16[4,64,128,128]{3,2,1,0:T(8,128)(2,1)}, /*index=5*/s32[]{:T(128)}, s32[]{:T(128)}) while((s32[]{:T(128)}, f32[64,128,128]{2,1,0:T(8,128)}, s32[]{:T(128)}, bf16[4,64]{1,0:T(4,128)(2,1)S(1)}, ...), condition=%wide.region_7.8_spmd.clone, body=%wide.region_6.7_spmd.clone.sunk | while | flops 5242948 | bytes 10486513 | solution.py:43
  215.1 4.6 %fusion.74 = f32[64,128,128]{2,1,0:T(8,128)} fusion(f32[64,128,128]{2,1,0:T(8,128)} %get-tuple-element.601, bf16[4,64,128,128]{3,2,1,0:T(8,128)(2,1)} %get-tuple-element.611, s32[]{:T(128)S(6)} %copy.210, f32[64]{0:T(128)S(1)} %bitcast_convert_fusion.5, pred[]{:T(512)S(6)} %compare.8, pred[]{:T(512)S(6)} %lt.47), kind=kLoop, calls=%fused_computation.4.clone.1 | loop fusion | flops 5242880 | bytes 10486022 | tf_op jit(solution)/shard_map/while/body/eval_jaxpr/jit(_where)/select_n | solution.py:41
  219.7 6.0 %fusion.74 = f32[64,128,128]{2,1,0:T(8,128)} fusion(f32[64,128,128]{2,1,0:T(8,128)} %get-tuple-element.601, bf16[4,64,128,128]{3,2,1,0:T(8,128)(2,1)} %get-tuple-element.611, s32[]{:T(128)S(6)} %copy.210, f32[64]{0:T(128)S(1)} %bitcast_convert_fusion.5, pred[]{:T(512)S(6)} %compare.8, pred[]{:T(512)S(6)} %lt.47), kind=kLoop, calls=%fused_computation.4.clone.1 | loop fusion | flops 5242880 | bytes 10486022 | tf_op jit(solution)/shard_map/while/body/eval_jaxpr/jit(_where)/select_n | solution.py:41
  225.7 5.9 %fusion.74 = f32[64,128,128]{2,1,0:T(8,128)} fusion(f32[64,128,128]{2,1,0:T(8,128)} %get-tuple-element.601, bf16[4,64,128,128]{3,2,1,0:T(8,128)(2,1)} %get-tuple-element.611, s32[]{:T(128)S(6)} %copy.210, f32[64]{0:T(128)S(1)} %bitcast_convert_fusion.5, pred[]{:T(512)S(6)} %compare.8, pred[]{:T(512)S(6)} %lt.47), kind=kLoop, calls=%fused_computation.4.clone.1 | loop fusion | flops 5242880 | bytes 10486022 | tf_op jit(solution)/shard_map/while/body/eval_jaxpr/jit(_where)/select_n | solution.py:41
  231.6 5.9 %fusion.74 = f32[64,128,128]{2,1,0:T(8,128)} fusion(f32[64,128,128]{2,1,0:T(8,128)} %get-tuple-element.601, bf16[4,64,128,128]{3,2,1,0:T(8,128)(2,1)} %get-tuple-element.611, s32[]{:T(128)S(6)} %copy.210, f32[64]{0:T(128)S(1)} %bitcast_convert_fusion.5, pred[]{:T(512)S(6)} %compare.8, pred[]{:T(512)S(6)} %lt.47), kind=kLoop, calls=%fused_computation.4.clone.1 | loop fusion | flops 5242880 | bytes 10486022 | tf_op jit(solution)/shard_map/while/body/eval_jaxpr/jit(_where)/select_n | solution.py:41
  237.6 2.8 convert_element_type.274
  241.2 2.7 fusion.10
  244.3 5.6 %fusion.7 = bf16[8192,512]{0,1:T(8,128)(2,1)} fusion(bf16[256,512]{0,1:T(8,128)(2,1)S(1)} %bitcast.154, bf16[1,256,8192]{2,1,0:T(8,128)(2,1)S(1)} %copy-done.1), kind=kOutput, calls=%fused_computation.16 | convolution fusion | flops 2151677952 | bytes 12845056 | tf_op jit(solution)/shard_map/dot_general | solution.py:162
  250.6 4.9 %multiply_reduce_fusion = f32[8192]{0:T(1024)S(1)} fusion(bf16[1,256,8192]{2,1,0:T(8,128)(2,1)} %param.13, bf16[1,256,8192]{2,1,0:T(8,128)(2,1)} %param.17), kind=kLoop, calls=%fused_computation.26 | loop fusion | flops 8380416 | bytes 8421376 | tf_op jit(solution)/shard_map/transpose(jvp())/while/body/eval_jaxpr/reduce_sum | solution.py:71
  255.6 62.8 %psum.15 = f32[64]{0:T(128)S(1)} all-reduce(f32[64]{0:T(128)S(1)} %reshape.381), channel_id=1, replica_groups=mesh['seq'=4,'fsdp'=16,'dp'=2] {'seq','fsdp','dp'}, use_global_device_ids=true, to_apply=%region_21.22 | all-reduce | flops 64 | bytes 512 | tf_op jit(solution)/shard_map/psum | solution.py:171
  319.1 7.3 %fusion.8 = bf16[4,16,256,128]{2,3,1,0:T(8,128)(2,1)} fusion(bf16[4,16,128,256]{3,2,1,0:T(8,128)(2,1)} %bitcast.143, f32[4,256,256]{2,1,0:T(8,128)} %copy-done.5, f32[4,16,256]{2,1,0:T(8,128)S(1)} %reduce_window_sum.59, pred[256,256]{1,0:T(8,128)(4,1)S(1)} %iota_compare_fusion), kind=kOutput, calls=%fused_computation.17 | convolution fusion | flops 1090519040 | bytes 9568256 | tf_op jit(solution)/shard_map/transpose(jvp())/while/body/eval_jaxpr/gkts,sgkp->tgkp/dot_general | solution.py:58
  326.5 23.1 %while.20 = (s32[]{:T(128)}, f32[64,128,128]{2,1,0:T(8,128)}, s32[]{:T(128)}, bf16[4,64]{1,0:T(4,128)(2,1)S(1)}, bf16[4,64,128,128]{3,2,1,0:T(8,128)(2,1)}, /*index=5*/s32[]{:T(128)}, s32[]{:T(128)}, s32[]{:T(128)}, s32[]{:T(128)}) while((s32[]{:T(128)}, f32[64,128,128]{2,1,0:T(8,128)}, s32[]{:T(128)}, ...), condition=%wide.region_3.4_spmd.clone, body=%wide.region_2.3_spmd.clone.sunk | while | flops 5242952 | bytes 10486575 | solution.py:43
  326.5 4.6 %fusion.73 = f32[64,128,128]{2,1,0:T(8,128)} fusion(f32[64,128,128]{2,1,0:T(8,128)} %get-tuple-element.576, bf16[4,64,128,128]{3,2,1,0:T(8,128)(2,1)} %get-tuple-element.588, s32[]{:T(128)S(6)} %select_n.103, f32[64]{0:T(128)S(1)} %bitcast_convert_fusion.4, pred[]{:T(512)S(6)} %compare.7, pred[]{:T(512)S(6)} %gt.12), kind=kLoop, calls=%fused_computation.1.clone.1 | loop fusion | flops 5242880 | bytes 10486022 | tf_op jit(solution)/shard_map/while/body/eval_jaxpr/jit(_where)/select_n | solution.py:41
  331.2 6.3 %fusion.73 = f32[64,128,128]{2,1,0:T(8,128)} fusion(f32[64,128,128]{2,1,0:T(8,128)} %get-tuple-element.576, bf16[4,64,128,128]{3,2,1,0:T(8,128)(2,1)} %get-tuple-element.588, s32[]{:T(128)S(6)} %select_n.103, f32[64]{0:T(128)S(1)} %bitcast_convert_fusion.4, pred[]{:T(512)S(6)} %compare.7, pred[]{:T(512)S(6)} %gt.12), kind=kLoop, calls=%fused_computation.1.clone.1 | loop fusion | flops 5242880 | bytes 10486022 | tf_op jit(solution)/shard_map/while/body/eval_jaxpr/jit(_where)/select_n | solution.py:41
  337.5 6.1 %fusion.73 = f32[64,128,128]{2,1,0:T(8,128)} fusion(f32[64,128,128]{2,1,0:T(8,128)} %get-tuple-element.576, bf16[4,64,128,128]{3,2,1,0:T(8,128)(2,1)} %get-tuple-element.588, s32[]{:T(128)S(6)} %select_n.103, f32[64]{0:T(128)S(1)} %bitcast_convert_fusion.4, pred[]{:T(512)S(6)} %compare.7, pred[]{:T(512)S(6)} %gt.12), kind=kLoop, calls=%fused_computation.1.clone.1 | loop fusion | flops 5242880 | bytes 10486022 | tf_op jit(solution)/shard_map/while/body/eval_jaxpr/jit(_where)/select_n | solution.py:41
  343.6 6.0 %fusion.73 = f32[64,128,128]{2,1,0:T(8,128)} fusion(f32[64,128,128]{2,1,0:T(8,128)} %get-tuple-element.576, bf16[4,64,128,128]{3,2,1,0:T(8,128)(2,1)} %get-tuple-element.588, s32[]{:T(128)S(6)} %select_n.103, f32[64]{0:T(128)S(1)} %bitcast_convert_fusion.4, pred[]{:T(512)S(6)} %compare.7, pred[]{:T(512)S(6)} %gt.12), kind=kLoop, calls=%fused_computation.1.clone.1 | loop fusion | flops 5242880 | bytes 10486022 | tf_op jit(solution)/shard_map/while/body/eval_jaxpr/jit(_where)/select_n | solution.py:41
  353.2 6.1 %fusion.12 = (f32[256,4,16]{0,2,1:T(8,128)}, bf16[256,4,128]{0,2,1:T(8,128)(2,1)}) fusion(f32[256,4,128]{0,2,1:T(8,128)S(1)} %copy-done.8, f32[256,4,16]{0,2,1:T(8,128)S(1)} %bitcast.161, bf16[4,16,128,128]{3,2,1,0:T(8,128)(2,1)S(1)} %bitcast.136, bf16[256,4,16,128]{3,2,1,0:T(8,128)(2,1)S(1)} %bitcast.148), kind=kOutput, calls=%fused_computation.25 | convolution fusion | flops 549306368 | bytes 7208960 | tf_op jit(solution)/shard_map/transpose(jvp())/while/body/eval_jaxpr/sgkp,sgkn->gkpn/dot_general | solution.py:66
  366.5 8.6 %fusion.21 = bf16[256,4,16,128]{0,3,2,1:T(8,128)(2,1)} fusion(bf16[256,4,16,128]{0,3,2,1:T(8,128)(2,1)} %bitcast.144, bf16[4,16,256,128]{2,3,1,0:T(8,128)(2,1)} %fusion.8, f32[4,16]{1,0:T(4,128)S(1)} %mul.237, bf16[4,16,128,128]{3,2,1,0:T(8,128)(2,1)} %bitcast.137, f32[256,4,16]{0,2,1:T(8,128)} %bitcast.160, f32[256,4,128]{0,2,1:T(8,128)} %copy-done.7), kind=kOutput, calls=%fused_computation.39 | convolution fusion | flops 553648128 | bytes 15270144 | tf_op jit(solution)/shard_map/transpose(jvp())/while/body/eval_jaxpr/sgkp,sgkn->gkpn/dot_general | solution.py:66
  375.3 6.3 %copy.175 = bf16[1,256,8192]{2,1,0:T(8,128)(2,1)} copy(bf16[1,256,8192]{1,2,0:T(8,128)(2,1)} %bitcast.149) | data formatting | bytes 8388608
  383.3 50.2 %all-reduce.4.cloned.1.call-done = bf16[512,512]{0,1:T(8,128)(2,1)} async-done(((bf16[512,512]{0,1:T(8,128)(2,1)}), bf16[512,512]{0,1:T(8,128)(2,1)}) %all-reduce.4.cloned.1.call-update) | async-done | bytes 524304 | tf_op jit(solution)/shard_map/psum | solution.py:169
  (107 shorter events, 24.2 us)
Async XLA Ops:
  7.2 207.9 %all-gather.6.cloned.1.call-start = ((), (), s32[]{:S(2)}) async-start(), calls=%async_computation.3 | async-start | bytes 10485760 | tf_op jit(solution)/shard_map/all_gather | solution.py:25
  10.4 3.7 copy-start.11
  10.4 3.6 copy-start.7
  14.0 4.9 %copy-start.3 = (bf16[32,8,64,128]{3,2,1,0:T(8,128)(2,1)}, bf16[32,8,64,128]{3,2,1,0:T(8,128)(2,1)S(1)}, u32[]{:S(2)}) copy-start(bf16[32,8,64,128]{3,2,1,0:T(8,128)(2,1)S(1)} %copy.186) | copy-start | bytes 12582916
  18.9 3.0 copy-start.6
  25.9 132.2 %all-to-all-start = ((bf16[16,512,512]{2,1,0:T(8,128)(2,1)}), bf16[16,512,512]{2,1,0:T(8,128)(2,1)}, u32[]{:S(2)}, u32[]{:S(2)}) async-start(bf16[16,512,512]{2,1,0:T(8,128)(2,1)} %stack.2), calls=%async_computation | async-start | bytes 16777216 | tf_op jit(solution)/shard_map/all_to_all | solution.py:18
  34.1 292.4 %all-gather.4.cloned.1.call-start = ((), (), s32[]{:S(2)}) async-start(), calls=%async_computation.2 | async-start | bytes 10485760 | tf_op jit(solution)/shard_map/all_gather | solution.py:25
  165.4 5.0 %copy-start.9 = (f32[256,4,128]{0,2,1:T(8,128)}, f32[256,4,128]{0,2,1:T(8,128)S(1)}, u32[]{:S(2)}) copy-start(f32[256,4,128]{0,2,1:T(8,128)S(1)} %copy.148) | copy-start | bytes 1572868
  170.4 4.3 copy-start.16
  174.5 200.7 %reduce-scatter.2.cloned.1.call-start = ((), (), s32[]{:S(2)}) async-start(), calls=%async_computation.4 | async-start | bytes 8912896 | tf_op jit(solution)/shard_map/reduce_scatter | solution.py:161
  197.6 1.0 copy-start.5
  237.6 3.5 copy-start.2
  237.6 3.6 copy-start.10
  241.2 3.0 copy-start.1
  249.8 0.7 copy-start.15
  249.8 183.7 %all-reduce.4.cloned.1.call-start = ((), (), s32[]{:S(2)}) async-start(), calls=%async_computation.5 | async-start | bytes 1048576 | tf_op jit(solution)/shard_map/psum | solution.py:169
  250.6 68.4 %copy-start.14 = (f32[4,16,256]{2,1,0:T(8,128)S(1)}, f32[4,16,256]{2,1,0:T(8,128)}, u32[]{:S(2)}) copy-start(f32[4,16,256]{2,1,0:T(8,128)} %get-tuple-element.473) | copy-start | bytes 196612
  319.1 7.3 %copy-start.13 = (f32[256,4,16]{0,2,1:T(8,128)S(1)}, f32[256,4,16]{0,2,1:T(8,128)}, u32[]{:S(2)}) copy-start(f32[256,4,16]{0,2,1:T(8,128)} %get-tuple-element.476) | copy-start | bytes 196612
  349.6 3.4 copy-start.4
  349.6 3.6 copy-start.8
  349.6 3.6 copy-start.12
  352.3 6.9 %copy-start = (bf16[64,128,128]{2,1,0:T(8,128)(2,1)}, bf16[64,128,128]{2,1,0:T(8,128)(2,1)S(1)}, u32[]{:S(2)}) copy-start(bf16[64,128,128]{2,1,0:T(8,128)(2,1)S(1)} %convert_element_type.255) | copy-start | bytes 6291460
Sparse Core Ops, SparseCore 0:
  22.0 85.5 all-gather.5
  174.6 83.2 all-gather.3
  261.3 86.4 reduce-scatter.1
  375.3 58.1 all-reduce.3
